TPU v7x, 256 devices: a whole 4x4x8 slice. The times are simulated.
256 devices in a mesh: op: 32 (over x, y, core), sec: 8 (over z).
Axes of the slice: x: 4, y: 4, z: 8, core: 2. Of those that a mesh axis runs over, the one named last changes fastest.
Arguments:
- wavefunction: bfloat16 [8192, 128], P(('op', 'sec')), may hold values from -6 to 6
- left_ops: bfloat16 [16384, 128, 128], P(('op', 'sec')), may hold values from -0.5 to 0.5
- right_ops: bfloat16 [16384, 128, 128], P(('op', 'sec')), may hold values from -0.0078125 to 0.0078125
- davidson_basis: bfloat16 [4, 64, 128, 128], P(None, 'sec'), may hold values from -0.005859375 to 0.005859375
- term_left: int32 [262144], P(('op', 'sec')), may hold values from 0 to 63
- term_right: int32 [262144], P(('op', 'sec')), may hold values from 0 to 63
- term_source: int32 [262144], P(('op', 'sec')), may hold values from 0 to 63
- term_target: int32 [262144], P(('op', 'sec')), may hold values from 0 to 7
- term_count: int32 [256], P(('op', 'sec')), may hold values from 256 to 1024, as said below
Outputs:
- sigma_blocks: float32 [64, 128, 128], P('sec')
- correlations: float32 [4], replicated
Inputs may be any that keep to these rules, and one draw needn't show every extreme that they name: `term_count`: some device has all 1024 slots live and some device has 256 live.
All inputs are finite; a program needn't handle non-finite values.
Results may differ from a plain program's by a relative error of at most 0.004.
Values may be sent and summed in bfloat16 or wider, within the bound.
A program may use at most 128 MiB of HBM per device.

v0:
```python
import jax
import jax.numpy as jnp
from jax import lax
from jax.sharding import PartitionSpec as P

TERM_BLOCK = 128


def build_partial(
    blocks,
    left_ops,
    right_ops,
    term_left,
    term_right,
    term_source,
    term_target,
    active_term_count,
    sec_dev,
):
    blk_width = left_ops.shape[1]
    num_blocks = (active_term_count + TERM_BLOCK - 1) // TERM_BLOCK
    slot_ids = jnp.arange(sec_dev, dtype=jnp.int32)

    def add_block(block_id, sigma_acc):
        first_term = block_id * TERM_BLOCK
        term_index = first_term + jnp.arange(TERM_BLOCK, dtype=jnp.int32)
        is_live = term_index < active_term_count
        left_operator_index = lax.dynamic_slice_in_dim(term_left, first_term, TERM_BLOCK)
        right_index = lax.dynamic_slice_in_dim(term_right, first_term, TERM_BLOCK)
        source_index = lax.dynamic_slice_in_dim(term_source, first_term, TERM_BLOCK)
        target_index = lax.dynamic_slice_in_dim(term_target, first_term, TERM_BLOCK)
        left_environment_blocks = jnp.take(left_ops, left_operator_index, axis=0)
        right_environment_blocks = jnp.take(right_ops, right_index, axis=0)
        source_sectors = jnp.take(blocks, source_index, axis=0)
        half_product = jnp.einsum(
            "esg,egu->esu",
            left_environment_blocks,
            source_sectors,
            preferred_element_type=jnp.float32,
        ).astype(jnp.bfloat16)
        term_products = jnp.einsum(
            "wfi,woi->wfo",
            half_product,
            right_environment_blocks,
            preferred_element_type=jnp.float32,
        )
        one_hot = ((target_index[:, None] == slot_ids[None, :]) & is_live[:, None]).astype(
            jnp.float32
        )
        return sigma_acc + jnp.einsum(
            "ts,tad->sad", one_hot, term_products, precision=lax.Precision.HIGHEST
        )

    empty_acc = jnp.zeros((sec_dev, blk_width, blk_width), jnp.float32)
    return lax.fori_loop(0, num_blocks, add_block, empty_acc)


def inner_products(basis_part, values):
    return jnp.einsum(
        "ksab,sab->k", basis_part.astype(jnp.float32), values, precision=lax.Precision.HIGHEST
    )


def body(
    wavefunction,
    left_ops,
    right_ops,
    davidson_basis,
    term_left,
    term_right,
    term_source,
    term_target,
    term_count,
):
    blk_width = left_ops.shape[1]
    sec_dev = davidson_basis.shape[1]
    all_rows = lax.all_gather(wavefunction, ("op", "sec"), axis=0, tiled=True)
    blocks = all_rows.reshape(-1, blk_width, blk_width)
    partial_value = build_partial(
        blocks,
        left_ops,
        right_ops,
        term_left,
        term_right,
        term_source,
        term_target,
        term_count[0],
        sec_dev,
    )
    sigma_blocks = lax.psum(partial_value, "op")
    correlations = lax.psum(inner_products(davidson_basis, sigma_blocks), "sec")
    return (sigma_blocks, correlations)


def solution(mesh):
    placed = (
        P(("op", "sec"), None),
        P(("op", "sec"), None, None),
        P(("op", "sec"), None, None),
        P(None, "sec", None, None),
        P(("op", "sec")),
        P(("op", "sec")),
        P(("op", "sec")),
        P(("op", "sec")),
        P(("op", "sec")),
    )
    return jax.shard_map(
        body, mesh=mesh, in_specs=placed, out_specs=(P("sec", None, None), P()), check_vma=False
    )
```

profile of v0, /device:TPU:1, one launch (start us, length us, event | category | flops | bytes accessed | tf_op | source)
XLA Modules:
  0.0 553.4 jit_solution(1699835773650587130)
XLA Ops:
  7.2 0.0 copy-start
  7.2 0.0 all-gather.2.cloned.1.call-start
  7.2 0.7 all-gather.2.cloned.1.call-update
  7.9 0.0 all-reduce.2.cloned.1.call-start
  8.6 111.3 %all-gather.2.cloned.1.call-done = bf16[8192,128]{1,0:T(8,128)(2,1)} async-done(((bf16[32,128]{1,0:T(8,128)(2,1)}), bf16[8192,128]{1,0:T(8,128)(2,1)}) %all-gather.2.cloned.1.call-update) | async-done | bytes 2097168 | tf_op jit(solution)/shard_map/all_gather | solution.py:77
  120.0 0.8 broadcast_in_dim.15
  120.8 108.8 %while.11 = (s32[]{:T(128)}, f32[8,128,128]{2,0,1:T(8,128)}, s32[]{:T(128)}, s32[1024]{0:T(1024)}, s32[]{:T(128)}, /*index=5*/s32[1024]{0:T(1024)}, bf16[64,128,...) while((s32[]{:T(128)}, f32[8,128,128]{2,0,1:T(8,128)}, ...), condition=%wide.region_1.3_spmd.clone, body=%wide.region_0.2_spmd.clone.sunk | while | flops 1283595776 | bytes 68178720 | solution.py:55
  120.8 0.8 dynamic_slice.23
  121.6 1.4 compare_and_fusion.6
  123.0 0.8 compare_and_fusion.5
  123.8 0.0 copy-start.1
  123.8 4.8 gather_fusion.1
  128.6 0.0 copy-done.1
  128.6 3.0 gather_fusion.2
  131.6 4.6 gather_fusion
  136.2 0.0 copy-start.2
  136.2 9.5 %fusion.49 = f32[128,128,128]{2,1,0:T(8,128)} fusion(bf16[128,128,128]{2,1,0:T(8,128)(2,1)} %gather_fusion, pred[128]{0:T(512)(128)(4,1)S(1)} %get-tuple-element.199, bf16[128,128,128]{2,1,0:T(8,128)(2,1)} %gather_fusion.1, bf16[128,128,128]{2,1,0:T(8,128)(2,1)} %gather_fusion.2, pred[128]{0:T(512)(128)(4,1)S(1)} %get-tuple-element.202, ...), kind=kOutput, calls=%fused_computation.6.clone.1 | convolution fusion | flops 1082130432 | bytes 20971904 | tf_op jit(solution)/shard_map/while/body/wfi,woi->wfo/dot_general | solution.py:41
  145.7 0.0 copy-done.2
  145.7 10.6 %fusion.50 = f32[8,128,128]{2,0,1:T(8,128)S(1)} fusion(f32[8,128,128]{2,0,1:T(8,128)S(1)} %copy-done.2, f32[128,128,128]{2,1,0:T(8,128)} %fusion.49, s32[128]{0:T(128)S(1)} %dynamic_slice.23, pred[128]{0:T(512)(128)(4,1)S(1)} %get-tuple-element.204), kind=kOutput, calls=%fused_computation.16.clone.1 | convolution fusion | flops 201459712 | bytes 9437824 | tf_op jit(solution)/shard_map/while/body/ts,tad->sad/dot_general | solution.py:50
  156.3 0.0 copy-start.3
  156.3 0.8 copy-done.3
  157.1 0.8 dynamic_slice.23
  157.8 1.4 compare_and_fusion.6
  159.2 0.8 compare_and_fusion.5
  160.1 0.0 copy-start.1
  160.1 4.8 gather_fusion.1
  164.8 0.0 copy-done.1
  164.8 3.0 gather_fusion.2
  167.8 4.6 gather_fusion
  172.5 0.0 copy-start.2
  172.5 9.5 %fusion.49 = f32[128,128,128]{2,1,0:T(8,128)} fusion(bf16[128,128,128]{2,1,0:T(8,128)(2,1)} %gather_fusion, pred[128]{0:T(512)(128)(4,1)S(1)} %get-tuple-element.199, bf16[128,128,128]{2,1,0:T(8,128)(2,1)} %gather_fusion.1, bf16[128,128,128]{2,1,0:T(8,128)(2,1)} %gather_fusion.2, pred[128]{0:T(512)(128)(4,1)S(1)} %get-tuple-element.202, ...), kind=kOutput, calls=%fused_computation.6.clone.1 | convolution fusion | flops 1082130432 | bytes 20971904 | tf_op jit(solution)/shard_map/while/body/wfi,woi->wfo/dot_general | solution.py:41
  182.0 0.0 copy-done.2
  182.0 10.6 %fusion.50 = f32[8,128,128]{2,0,1:T(8,128)S(1)} fusion(f32[8,128,128]{2,0,1:T(8,128)S(1)} %copy-done.2, f32[128,128,128]{2,1,0:T(8,128)} %fusion.49, s32[128]{0:T(128)S(1)} %dynamic_slice.23, pred[128]{0:T(512)(128)(4,1)S(1)} %get-tuple-element.204), kind=kOutput, calls=%fused_computation.16.clone.1 | convolution fusion | flops 201459712 | bytes 9437824 | tf_op jit(solution)/shard_map/while/body/ts,tad->sad/dot_general | solution.py:50
  192.5 0.0 copy-start.3
  192.6 0.8 copy-done.3
  193.3 0.8 dynamic_slice.23
  194.1 1.4 compare_and_fusion.6
  195.5 0.8 compare_and_fusion.5
  196.3 0.0 copy-start.1
  196.3 4.8 gather_fusion.1
  201.1 0.0 copy-done.1
  201.1 3.0 gather_fusion.2
  204.1 4.6 gather_fusion
  208.8 0.0 copy-start.2
  208.8 9.5 %fusion.49 = f32[128,128,128]{2,1,0:T(8,128)} fusion(bf16[128,128,128]{2,1,0:T(8,128)(2,1)} %gather_fusion, pred[128]{0:T(512)(128)(4,1)S(1)} %get-tuple-element.199, bf16[128,128,128]{2,1,0:T(8,128)(2,1)} %gather_fusion.1, bf16[128,128,128]{2,1,0:T(8,128)(2,1)} %gather_fusion.2, pred[128]{0:T(512)(128)(4,1)S(1)} %get-tuple-element.202, ...), kind=kOutput, calls=%fused_computation.6.clone.1 | convolution fusion | flops 1082130432 | bytes 20971904 | tf_op jit(solution)/shard_map/while/body/wfi,woi->wfo/dot_general | solution.py:41
  218.2 0.0 copy-done.2
  218.2 10.6 %fusion.50 = f32[8,128,128]{2,0,1:T(8,128)S(1)} fusion(f32[8,128,128]{2,0,1:T(8,128)S(1)} %copy-done.2, f32[128,128,128]{2,1,0:T(8,128)} %fusion.49, s32[128]{0:T(128)S(1)} %dynamic_slice.23, pred[128]{0:T(512)(128)(4,1)S(1)} %get-tuple-element.204), kind=kOutput, calls=%fused_computation.16.clone.1 | convolution fusion | flops 201459712 | bytes 9437824 | tf_op jit(solution)/shard_map/while/body/ts,tad->sad/dot_general | solution.py:50
  228.8 0.0 copy-start.3
  228.8 0.8 copy-done.3
  229.6 1.9 copy.11
  231.6 0.0 all-reduce.2.cloned.1.call-update
  231.6 293.5 %all-reduce.2.cloned.1.call-done = f32[8,128,128]{2,1,0:T(8,128)} async-done(((f32[8,128,128]{2,1,0:T(8,128)}), f32[8,128,128]{2,1,0:T(8,128)}) %all-reduce.2.cloned.1.call-update) | async-done | bytes 524304 | tf_op jit(solution)/shard_map/psum | solution.py:90
  525.1 0.0 copy-start.4
  525.1 0.0 copy-done
  525.1 6.5 %convolution_bitcast_fusion = f32[4]{0:T(128)S(1)} fusion(bf16[4,8,128,128]{3,2,1,0:T(8,128)(2,1)S(1)} %copy-done, f32[8,128,128,1]{2,1,0,3:T(8,128)} %bitcast.14), kind=kOutput, calls=%fused_computation.33 | convolution fusion | flops 6291456 | bytes 1572880 | tf_op jit(solution)/shard_map/ksab,sab->k/dot_general | solution.py:59
  531.6 14.2 %psum.15 = f32[4]{0:T(128)} all-reduce(f32[4]{0:T(128)S(1)} %convolution_bitcast_fusion), channel_id=1, replica_groups=mesh['op'=32,'sec'=8] {'sec'}, use_global_device_ids=true, to_apply=%region_3.5 | all-reduce | flops 4 | bytes 32 | tf_op jit(solution)/shard_map/psum | solution.py:91
  545.8 0.0 copy-done.4
  545.8 0.8 copy.34
  (9 shorter events, 0.1 us)
Async XLA Ops:
  7.2 518.0 %copy-start = (bf16[4,8,128,128]{3,2,1,0:T(8,128)(2,1)S(1)}, bf16[4,8,128,128]{3,2,1,0:T(8,128)(2,1)}, u32[]{:S(2)}) copy-start(bf16[4,8,128,128]{3,2,1,0:T(8,128)(2,1)} %param.16) | copy-start | bytes 3145732
  7.2 112.8 %all-gather.2.cloned.1.call-start = ((), (), s32[]{:S(2)}) async-start(), calls=%async_computation | async-start | bytes 2105344 | tf_op jit(solution)/shard_map/all_gather | solution.py:77
  7.9 517.2 %all-reduce.2.cloned.1.call-start = ((), (), s32[]{:S(2)}) async-start(), calls=%async_computation.1 | async-start | bytes 1048576 | tf_op jit(solution)/shard_map/psum | solution.py:90
  123.8 4.8 copy-start.1
  136.2 9.5 %copy-start.2 = (f32[8,128,128]{2,0,1:T(8,128)S(1)}, f32[8,128,128]{2,0,1:T(8,128)}, u32[]{:S(2)}) copy-start(f32[8,128,128]{2,0,1:T(8,128)} %get-tuple-element.221) | copy-start | bytes 1572868 | tf_op jit(solution)/shard_map/while
  156.3 0.8 copy-start.3
  160.1 4.8 copy-start.1
  172.5 9.5 %copy-start.2 = (f32[8,128,128]{2,0,1:T(8,128)S(1)}, f32[8,128,128]{2,0,1:T(8,128)}, u32[]{:S(2)}) copy-start(f32[8,128,128]{2,0,1:T(8,128)} %get-tuple-element.221) | copy-start | bytes 1572868 | tf_op jit(solution)/shard_map/while
  192.5 0.8 copy-start.3
  196.3 4.8 copy-start.1
  208.8 9.5 %copy-start.2 = (f32[8,128,128]{2,0,1:T(8,128)S(1)}, f32[8,128,128]{2,0,1:T(8,128)}, u32[]{:S(2)}) copy-start(f32[8,128,128]{2,0,1:T(8,128)} %get-tuple-element.221) | copy-start | bytes 1572868 | tf_op jit(solution)/shard_map/while
  228.8 0.8 copy-start.3
  525.1 20.7 %copy-start.4 = (f32[8,128,128]{2,1,0:T(8,128)S(1)}, f32[8,128,128]{2,1,0:T(8,128)}, u32[]{:S(2)}) copy-start(f32[8,128,128]{2,1,0:T(8,128)} %all-reduce.2.cloned.1.call-done) | copy-start | bytes 1572868
Sparse Core Ops, SparseCore 0:
  11.7 108.1 all-gather.1
  231.7 293.3 all-reduce.1
where the time goes:
time: 558 us; the launch traced here: 553 us
  waiting for transfers between devices  406 us (73%)
  matrix products  66.6 us (12%)
  local copies, waits for them, and re-layouts  45.5 us (8%)
  between operations  14.7 us (3%)
  blocking collectives  14.2 us (3%)
  other arithmetic  6.63 us (1%)
    psum x1, waiting for transfers between devices, body(): sigma_blocks = lax.psum(partial_value, 'op')  294 us
    all_gather x1, waiting for transfers between devices, body(): all_rows = lax.all_gather(wavefunction, ('op', 'sec'), axis=0, tiled=True)  111 us
    dot_general x3, matrix products, add_block(): jnp.einsum('ts,tad->sad', one_hot, term_products, precision=lax.Precision...  31.7 us
    dot_general x3, matrix products, add_block(): jnp.einsum('wfi,woi->wfo', half_product, right_environment_blocks, prefer...  28.4 us
    gather x3, local copies, waits for them, and re-layouts, add_block(): source_sectors = jnp.take(blocks, source_index, axis=0)  14.3 us
    psum x1, blocking collectives, body(): correlations = lax.psum(inner_products(davidson_basis, sigma_blocks), 'sec')  14.2 us
    gather x3, local copies, waits for them, and re-layouts, add_block(): right_environment_blocks = jnp.take(right_ops, right_index, axis=0)  13.9 us
  transfers between devices with their start and end apart: 2, of which 2 were waited for; matrix products, arithmetic and copies ran while one was open for 0% of the time, Pallas kernels for 0%

commit v1 on v0

v1 whole, which is shorter than its diff:
```python
import functools

import jax
import jax.numpy as jnp
from jax import lax
from jax.experimental import pallas as pl
from jax.experimental.pallas import tpu as pltpu
from jax.sharding import PartitionSpec as P

MESH = pl.DeviceIdType.MESH
BF, F32, I32 = jnp.bfloat16, jnp.float32, jnp.int32
SLOTS = 1024
CHUNK = 8
CHUNKS = 136
NT = (((1,), (1,)), ((), ()))


def remote(src, dst, send_sem, recv_sem, to):
    return pltpu.make_async_remote_copy(
        src_ref=src,
        dst_ref=dst,
        send_sem=send_sem,
        recv_sem=recv_sem,
        device_id=to,
        device_id_type=MESH,
    )


def fold(mask_or_value):
    return jnp.sum(mask_or_value.reshape(16, 8, 128), axis=0)


def sort_terms(tl, tr, ts, tt, count):
    row = lax.broadcasted_iota(I32, (8, 128), 0)
    lane = lax.broadcasted_iota(I32, (8, 128), 1)
    slot = row * 128 + lane
    live = slot < count
    rank_key = jnp.where(live, tt, 8) * SLOTS + slot
    value = (slot + 1) | (tr << 11)
    key_t, value_t = rank_key.T, value.T
    ranks = [jnp.zeros((8, 128), I32) for _ in range(8)]
    for j in range(8):
        key_j = jnp.broadcast_to(key_t[:, j : j + 1], (128, 128))
        for i in range(8):
            ranks[i] = ranks[i] + fold((key_j < rank_key[i : i + 1, :]).astype(I32))
    rank = jnp.concatenate([jnp.sum(r, axis=0, keepdims=True) for r in ranks], axis=0)
    base = jnp.zeros((1, 1), I32)
    start = jnp.zeros((1, 1), I32)
    place = jnp.where(live, rank, 1 << 20)
    restart = jnp.zeros((8, 128), I32)
    last = jnp.full((8, 128), CHUNKS, I32)
    for t in range(8):
        hit = live & (tt == t)
        n = jnp.sum(jnp.sum(hit.astype(I32), axis=0, keepdims=True), axis=1, keepdims=True)
        place = place + jnp.where(hit, start - base, 0)
        restart = restart | ((start == slot * CHUNK) & (n > 0)).astype(I32)
        base = base + n
        start = start + (((n + CHUNK - 1) >> 3) << 3)
        last = jnp.where((lane == t) & (n > 0), (start >> 3) - 1, last)
    place_t = place.T
    tables = [jnp.zeros((8, 128), I32) for _ in range(9)]
    for j in range(8):
        place_j = jnp.broadcast_to(place_t[:, j : j + 1], (128, 128))
        value_j = jnp.broadcast_to(value_t[:, j : j + 1], (128, 128))
        for i in range(9):
            at = lax.broadcasted_iota(I32, (128, 128), 1) + i * 128
            tables[i] = tables[i] + fold(jnp.where(place_j == at, value_j, 0))
    tables = [jnp.sum(t, axis=0, keepdims=True) for t in tables]
    tail = jnp.concatenate([tables[8], jnp.zeros((7, 128), I32)], axis=0)
    ends = jnp.where(row < 2, 1 - restart, last)
    return tl | (ts << 6), jnp.concatenate(tables[:8], axis=0), tail, ends


def kernel(
    w_ref,
    left_hbm,
    right_hbm,
    basis_hbm,
    tl_ref,
    tr_ref,
    ts_ref,
    tt_ref,
    count_ref,
    sigma_ref,
    corr_ref,
    xb,
    left,
    right,
    basis,
    half,
    sums,
    tab_v,
    tab_s,
    sig,
    part,
    inbox,
    outbox,
    corr_z,
    corr_p,
    local_sem,
    ag_send,
    ag_recv,
    rs_send,
    rs_recv,
    out_send,
    out_recv,
    cz_send,
    cz_recv,
    cp_send,
    cp_recv,
):
    op = lax.axis_index("op")
    z = lax.axis_index("sec")
    x, y, c = op // 8, (op // 2) % 4, op % 2

    def at(xx, yy, cc, zz):
        return {"op": (xx * 4 + yy) * 2 + cc, "sec": zz}

    z_peers = [at(x, y, c, (z + k) % 8) for k in range(1, 8)]
    y_peers = [at(x, (y + k) % 4, c, z) for k in range(1, 4)]
    x_peers = [at((x + k) % 4, y, c, z) for k in range(1, 4)]
    plane = [{"op": (op + k) % 32, "sec": z} for k in range(1, 32)]
    twin = at(x, y, 1 - c, z)

    barrier = pltpu.get_barrier_semaphore()
    for peer in z_peers + plane:
        pl.semaphore_signal(barrier, inc=1, device_id=peer, device_id_type=MESH)

    mine = xb.at[x, y, 2 * c + z // 4, pl.ds(pl.multiple_of((z % 4) * 32, 32), 32)]
    loads = [
        pltpu.make_async_copy(w_ref, mine, local_sem.at[0]),
        pltpu.make_async_copy(right_hbm, right, local_sem.at[1]),
        pltpu.make_async_copy(left_hbm, left, local_sem.at[2]),
        pltpu.make_async_copy(basis_hbm, basis, local_sem.at[3]),
    ]
    for load in loads:
        load.start()
    tables = sort_terms(tl_ref[...], tr_ref[...], ts_ref[...], tt_ref[...], count_ref[0])
    for i, table in enumerate(tables):
        tab_v[i] = table
    to_smem = pltpu.make_async_copy(tab_v, tab_s, local_sem.at[4])
    to_smem.start()
    half[0] = jnp.zeros((128, 128), BF)
    sums[CHUNKS] = jnp.zeros((128, 128), F32)
    to_smem.wait()
    for load in loads:
        load.wait()
    pl.semaphore_wait(barrier, 38)

    copies = []

    def push(src, to):
        i = len(copies)
        copy = remote(src, src, ag_send.at[i], ag_recv.at[i], to)
        copy.start()
        copies.append(copy)
        return copy

    first = [push(mine, peer) for peer in z_peers]
    for copy in first:
        copy.wait_recv()
    lo, hi = xb.at[x, y, 2 * c], xb.at[x, y, 2 * c + 1]
    along_y = [push(lo, peer) for peer in y_peers]
    along_x = [push(hi, peer) for peer in x_peers]
    relayed = [push(xb.at[x, y, pl.ds(2 * c, 2)], twin)]
    for copy in along_y + along_x:
        copy.wait_recv()
    row, column = xb.at[x, :, 2 * c], xb.at[:, y, 2 * c + 1]
    rows = [push(row, peer) for peer in x_peers]
    columns = [push(column, peer) for peer in y_peers]
    for k in range(1, 4):
        relayed.append(push(xb.at[x, (y + k) % 4, 2 * c], twin))
        relayed.append(push(xb.at[(x + k) % 4, y, 2 * c + 1], twin))
    for k in (0, 2, 1):
        rows[k].wait_recv()
        relayed.append(push(xb.at[(x + 3 - k) % 4, :, 2 * c], twin))
        columns[k].wait_recv()
        relayed.append(push(xb.at[:, (y + 3 - k) % 4, 2 * c + 1], twin))
    for copy in relayed:
        copy.wait_recv()

    def products(i, carry):
        for u in range(128):
            word = tab_s[0, i, u]
            l, s = word & 63, (word >> 6) & 63
            block = xb[s >> 4, (s >> 2) & 3, s & 3]
            half[i * 128 + u + 1] = jnp.dot(left[l], block, preferred_element_type=F32).astype(BF)
        return carry

    lax.fori_loop(0, SLOTS // 128, products, 0)

    def chunk_sums(i, acc):
        for v in range(17):
            chunk = i * 17 + v
            words = []
            for k in range(CHUNK):
                slot = chunk * CHUNK + k
                words.append(tab_s[1 + (slot >> 10), (slot >> 7) & 7, slot & 127])
            halves = jnp.concatenate([half[w & 2047] for w in words], axis=1)
            rights = jnp.concatenate([right[w >> 11] for w in words], axis=1)
            prod = lax.dot_general(halves, rights, NT, preferred_element_type=F32)
            keep = tab_s[3, chunk >> 7, chunk & 127]
            acc = acc * keep.astype(F32) + prod
            sums[chunk] = acc
        return acc

    lax.fori_loop(0, CHUNKS // 17, chunk_sums, jnp.zeros((128, 128), F32))

    def targets(p, carry):
        for h in range(2):
            total = sums[tab_s[3, 2, 2 * p + h]]
            sig[2 * p + h] = total
            part[p, 4 * h : 4 * h + 4] = total.astype(BF).reshape(4, 32, 128)
        for k in range(8):
            xo, co = (x + k // 2) % 4, (c + k) % 2
            yo = (p - xo + 4) % 4
            owner = (xo * 4 + yo) * 2 + co
            index = (op - owner + 31) % 32
            copy = remote(
                part.at[p, xo * 2 + co],
                inbox.at[index],
                rs_send,
                rs_recv,
                {"op": owner, "sec": z},
            )
            if k == 0:
                pl.when(owner != op)(copy.start)
            else:
                copy.start()
        return carry

    lax.fori_loop(0, 4, targets, 0)

    inner_sums = []
    for k in range(4):
        def inner(b, acc, k=k):
            prod = basis[k, b].astype(F32) * sig[b]
            return acc + jnp.sum(prod.reshape(16, 8, 128), axis=0)

        total = lax.fori_loop(0, 8, inner, jnp.zeros((8, 128), F32))
        inner_sums.append(jnp.sum(total, axis=0, keepdims=True))
    corr_z[z] = jnp.concatenate(inner_sums + [jnp.zeros((4, 128), F32)], axis=0)
    to_z = []
    for k, peer in enumerate(z_peers):
        copy = remote(corr_z.at[z], corr_z.at[z], cz_send.at[k], cz_recv.at[k], peer)
        copy.start()
        to_z.append(copy)

    whole = remote(inbox, inbox, rs_send, rs_recv, twin)
    whole.wait_recv()
    p_me, m_me = (x + y) % 4, x * 2 + c
    total = part[p_me, m_me].astype(F32)
    for k in range(31):
        total = total + inbox[k].astype(F32)
    t_me, r_me = 2 * p_me + m_me // 4, pl.multiple_of((m_me % 4) * 32, 32)
    out_mine = outbox.at[t_me, pl.ds(r_me, 32)]
    out_mine[...] = total.astype(BF)
    to_out = []
    for k, peer in enumerate(plane):
        copy = remote(out_mine, out_mine, out_send.at[k], out_recv.at[k], peer)
        copy.start()
        to_out.append(copy)

    for copy in to_z:
        copy.wait_recv()
    z_sum = corr_z[0]
    for k in range(1, 8):
        z_sum = z_sum + corr_z[k]
    corr_p[op] = z_sum
    to_plane = []
    for k, peer in enumerate(plane):
        copy = remote(corr_p.at[op], corr_p.at[op], cp_send.at[k], cp_recv.at[k], peer)
        copy.start()
        to_plane.append(copy)

    for copy in to_out:
        copy.wait_recv()
    sigma_ref[...] = outbox[...]
    for copy in to_plane:
        copy.wait_recv()
    p_sum = corr_p[0]
    for k in range(1, 32):
        p_sum = p_sum + corr_p[k]
    corr_ref[...] = jnp.broadcast_to(jnp.sum(p_sum, axis=1, keepdims=True), (8, 128))

    for copy in copies + to_z + to_out + to_plane:
        copy.wait_send()
    whole.wait_send()


def body(wavefunction, left_ops, right_ops, basis, tl, tr, ts, tt, count):
    vmem = pl.BlockSpec(memory_space=pltpu.VMEM)
    smem = pl.BlockSpec(memory_space=pltpu.SMEM)
    hbm = pl.BlockSpec(memory_space=pl.ANY)
    dma = pltpu.SemaphoreType.DMA
    sigma, corr = pl.pallas_call(
        kernel,
        out_shape=(
            jax.ShapeDtypeStruct((8, 128, 128), BF),
            jax.ShapeDtypeStruct((8, 128), F32),
        ),
        in_specs=[vmem, hbm, hbm, hbm, vmem, vmem, vmem, vmem, smem],
        out_specs=(vmem, vmem),
        scratch_shapes=[
            pltpu.VMEM((4, 4, 4, 128, 128), BF),
            pltpu.VMEM((64, 128, 128), BF),
            pltpu.VMEM((64, 128, 128), BF),
            pltpu.VMEM((4, 8, 128, 128), BF),
            pltpu.VMEM((SLOTS + 1, 128, 128), BF),
            pltpu.VMEM((CHUNKS + 1, 128, 128), F32),
            pltpu.VMEM((4, 8, 128), I32),
            pltpu.SMEM((4, 8, 128), I32),
            pltpu.VMEM((8, 128, 128), F32),
            pltpu.VMEM((4, 8, 32, 128), BF),
            pltpu.VMEM((31, 32, 128), BF),
            pltpu.VMEM((8, 128, 128), BF),
            pltpu.VMEM((8, 8, 128), F32),
            pltpu.VMEM((32, 8, 128), F32),
            dma((5,)),
            dma((32,)),
            dma((32,)),
            dma(()),
            dma(()),
            dma((31,)),
            dma((31,)),
            dma((7,)),
            dma((7,)),
            dma((31,)),
            dma((31,)),
        ],
        compiler_params=pltpu.CompilerParams(
            collective_id=0, has_side_effects=True, vmem_limit_bytes=60 * 1024 * 1024
        ),
    )(
        wavefunction,
        left_ops,
        right_ops,
        basis,
        *(t.reshape(8, 128) for t in (tl, tr, ts, tt)),
        count,
    )
    return sigma.astype(F32), corr[:4, 0]


def solution(mesh):
    placed = (
        P(("op", "sec"), None),
        P(("op", "sec"), None, None),
        P(("op", "sec"), None, None),
        P(None, "sec", None, None),
        P(("op", "sec")),
        P(("op", "sec")),
        P(("op", "sec")),
        P(("op", "sec")),
        P(("op", "sec")),
    )
    return jax.shard_map(
        body, mesh=mesh, in_specs=placed, out_specs=(P("sec", None, None), P()), check_vma=False
    )
```

time: 558 us -> 71.2 us (0.13)
  waiting for transfers between devices: 406 us -> 0 us
  matrix products: 66.6 us -> 0 us
  Pallas kernels: 0 us -> 66.6 us
  local copies, waits for them, and re-layouts: 45.5 us -> 1.3 us
  blocking collectives: 14.2 us -> 0 us
  between operations: 14.7 us -> 1.29 us
    psum x1 -> x0, waiting for transfers between devices: 294 us -> none  [body(): sigma_blocks = lax.psum(partial_value, 'op')]
    all_gather x1 -> x0, waiting for transfers between devices: 111 us -> none  [body(): all_rows = lax.all_gather(wavefunction, ('op', 'sec'), axis=0, tiled=True)]
    pallas_call x0 -> x1, Pallas kernels: none -> 66.6 us  [body(): pl.pallas_call(kernel, out_shape=(jax.ShapeDtypeStruct((8, 128, 128), BF)...]
    dot_general x7 -> x0, matrix products: 66.6 us -> none  [the longest x3 31.7 us: add_block(): jnp.einsum('ts,tad->sad', one_hot, term_products, precision=lax.Precision...]
    gather x9 -> x0, local copies, waits for them, and re-layouts: 37.2 us -> none  [the longest x3 14.3 us: add_block(): source_sectors = jnp.take(blocks, source_index, axis=0)]
    psum x1 -> x0, blocking collectives: 14.2 us -> none  [body(): correlations = lax.psum(inner_products(davidson_basis, sigma_blocks), 'sec')]
    and x6 -> x0, other arithmetic: 6.58 us -> none  [the longest x3 4.24 us: add_block(): left_environment_blocks = jnp.take(left_ops, left_operator_index, axis=0)]
  transfers between devices with their start and end apart: 2 -> 0, of which waited for: 2 -> 0; matrix products, arithmetic and copies ran while one was open for 0% -> 0% of each run, Pallas kernels for 0% -> 0%
where the time goes in v1:
time: 71.2 us; the launch traced here: 71 us
  Pallas kernels  66.6 us (94%)
  other arithmetic  1.78 us (2%)
  local copies, waits for them, and re-layouts  1.3 us (2%)
  between operations  1.29 us (2%)
    pallas_call x1, Pallas kernels, body(): pl.pallas_call(kernel, out_shape=(jax.ShapeDtypeStruct((8, 128, 128), BF)...  66.6 us
    convert_element_type x1, other arithmetic, body(): return (sigma.astype(F32), corr[:4, 0])  1.78 us

profile of v1, /device:TPU:1, one launch (start us, length us, event | category | flops | bytes accessed | tf_op | source)
XLA Modules:
  0.0 71.0 jit_solution(2299628195111086698)
XLA Ops:
  1.3 66.6 %shard_map.104 = (bf16[8,128,128]{2,1,0:T(8,128)(2,1)}, f32[8,128]{1,0:T(8,128)}) custom-call(bf16[32,128]{1,0:T(8,128)(2,1)} %w_ref.1, bf16[64,128,128]{2,1,0:T(8,128)(2,1)} %left_hbm.1, bf16[64,128,128]{2,1,0:T(8,128)(2,1)} %right_hbm.1, bf16[4,8,128,128]{3,2,1,0:T(8,128)(2,1)} %basis_hbm.1, s32[8,128]{1,0:T(8,128)} %bitcast.4, s32[8,128]{1,0:T(8,128)} %bitcast.5, ...), custom_call_target="tpu_custom_call" | custom-call | tf_op jit(solution)/shard_map/pallas_call | solution.py:296
  67.9 1.3 %slice_reduce_fusion = f32[4]{0:T(128)} fusion(f32[8,128]{1,0:T(8,128)} %get-tuple-element.5), kind=kLoop, calls=%fused_computation | loop fusion | bytes 32 | tf_op jit(solution)/shard_map/slice | solution.py:342
  69.2 1.8 %convert_element_type.3 = f32[8,128,128]{2,1,0:T(8,128)} convert(bf16[8,128,128]{2,1,0:T(8,128)(2,1)} %get-tuple-element.4) | non-fusion elementwise | flops 131072 | bytes 786432 | tf_op jit(solution)/shard_map/convert_element_type | solution.py:342

commit v2 on v1

v2 whole, which is shorter than its diff:
```python
import functools

import jax
import jax.numpy as jnp
from jax import lax
from jax.experimental import pallas as pl
from jax.experimental.pallas import tpu as pltpu
from jax.sharding import PartitionSpec as P

MESH = pl.DeviceIdType.MESH
BF, F32, I32 = jnp.bfloat16, jnp.float32, jnp.int32
SLOTS = 1024
CHUNK = 8
CHUNKS = 136
STAGED = ((304, 392, 328), (44, 78, 108, 136))
GENERAL = ((0, 0, 1024), (136, 136, 136, 136))
NT = (((1,), (1,)), ((), ()))


def remote(src, dst, send_sem, recv_sem, to):
    return pltpu.make_async_remote_copy(
        src_ref=src,
        dst_ref=dst,
        send_sem=send_sem,
        recv_sem=recv_sem,
        device_id=to,
        device_id_type=MESH,
    )


def fold(mask_or_value):
    return jnp.sum(mask_or_value.reshape(16, 8, 128), axis=0)


def ranks_of(key):
    key_t = key.T
    ranks = [jnp.zeros((8, 128), I32) for _ in range(8)]
    for j in range(8):
        key_j = jnp.broadcast_to(key_t[:, j : j + 1], (128, 128))
        for i in range(8):
            ranks[i] = ranks[i] + fold((key_j < key[i : i + 1, :]).astype(I32))
    return jnp.concatenate([jnp.sum(r, axis=0, keepdims=True) for r in ranks], axis=0)


def scatter(place, value, rows):
    place_t, value_t = place.T, value.T
    tables = [jnp.zeros((8, 128), I32) for _ in range(rows)]
    for j in range(8):
        place_j = jnp.broadcast_to(place_t[:, j : j + 1], (128, 128))
        value_j = jnp.broadcast_to(value_t[:, j : j + 1], (128, 128))
        for i in range(rows):
            at = lax.broadcasted_iota(I32, (128, 128), 1) + i * 128
            tables[i] = tables[i] + fold(jnp.where(place_j == at, value_j, 0))
    return [jnp.sum(t, axis=0, keepdims=True) for t in tables]


def count_of(mask):
    return jnp.sum(jnp.sum(mask.astype(I32), axis=0, keepdims=True), axis=1, keepdims=True)


def sort_terms(tl, tr, ts, tt, count, x, y, plan):
    row = lax.broadcasted_iota(I32, (8, 128), 0)
    lane = lax.broadcasted_iota(I32, (8, 128), 1)
    slot = row * 128 + lane
    live = slot < count

    dx, dy, odd = ((ts >> 4) - x) & 3, ((ts >> 2) - y) & 3, (ts & 1) == 1
    near, far = jnp.where(odd, dx, dy), jnp.where(odd, dy, dx)
    late = jnp.where((far == 0) | (near == 0), 0, 1)
    late = jnp.where(far == 2, 2, late)
    stages, marks = plan
    spot = ranks_of(jnp.where(live, late, 3) * SLOTS + slot)
    done, end = jnp.zeros((1, 1), I32), jnp.zeros((1, 1), I32)
    for i in range(3):
        n = count_of(live & (late == i))
        begin = jnp.maximum(end, sum(stages[:i]))
        spot = spot + jnp.where(late == i, begin - done, 0)
        done, end = done + n, begin + n
    over = jnp.maximum(end - SLOTS, 0)
    spot = jnp.where(live, spot, 1 << 20)
    first = jnp.concatenate(scatter(spot, tl | (ts << 6), 8), axis=0)
    spot = jnp.minimum(spot, SLOTS - 1)

    rank = ranks_of(jnp.where(live, tt, 8) * SLOTS + slot)
    base = jnp.zeros((1, 1), I32)
    start = jnp.zeros((1, 1), I32)
    place = jnp.where(live, rank, 1 << 20)
    restart = jnp.zeros((8, 128), I32)
    last = jnp.full((8, 128), CHUNKS, I32)
    for t in range(8):
        hit = live & (tt == t)
        n = count_of(hit)
        place = place + jnp.where(hit, start - base, 0)
        restart = restart | ((start == slot * CHUNK) & (n > 0)).astype(I32)
        base = base + n
        start = start + (((n + CHUNK - 1) >> 3) << 3)
        last = jnp.where((lane == t) & (n > 0), (start >> 3) - 1, last)
        over = jnp.maximum(over, start - CHUNK * marks[t // 2])
    tables = scatter(place, (spot + 1) | (tr << 11), 9)
    tail = jnp.concatenate([tables[8], jnp.zeros((7, 128), I32)], axis=0)
    ends = jnp.where(row < 2, 1 - restart, last)
    return first, jnp.concatenate(tables[:8], axis=0), tail, ends, over


def kernel(
    plan,
    w_ref,
    left_hbm,
    right_hbm,
    basis_hbm,
    tl_ref,
    tr_ref,
    ts_ref,
    tt_ref,
    count_ref,
    sigma_ref,
    corr_ref,
    over_ref,
    xb1,
    xb2,
    xb3,
    left,
    right,
    basis,
    half,
    sums,
    tab_v,
    tab_s,
    sig,
    part,
    inbox,
    outbox,
    corr_z,
    corr_p,
    local_sem,
    ag_send,
    ag_recv,
    rs_send,
    rs_recv,
    out_send,
    out_recv,
    cz_send,
    cz_recv,
    cp_send,
    cp_recv,
):
    op = lax.axis_index("op")
    z = lax.axis_index("sec")
    x, y, c = op // 8, (op // 2) % 4, op % 2

    def at(xx, yy, cc, zz):
        return {"op": (xx * 4 + yy) * 2 + cc, "sec": zz}

    z_peers = [at(x, y, c, (z + k) % 8) for k in range(1, 8)]
    y_peers = [at(x, (y + k) % 4, c, z) for k in range(1, 4)]
    x_peers = [at((x + k) % 4, y, c, z) for k in range(1, 4)]
    plane = [{"op": (op + k) % 32, "sec": z} for k in range(1, 32)]
    twin = at(x, y, 1 - c, z)

    barrier = pltpu.get_barrier_semaphore()
    for peer in z_peers + plane:
        pl.semaphore_signal(barrier, inc=1, device_id=peer, device_id_type=MESH)

    stages, marks = plan
    mine = xb1.at[x, y, c, z // 4, pl.ds(pl.multiple_of((z % 4) * 32, 32), 32)]
    loads = [
        pltpu.make_async_copy(w_ref, mine, local_sem.at[0]),
        pltpu.make_async_copy(right_hbm, right, local_sem.at[1]),
        pltpu.make_async_copy(left_hbm, left, local_sem.at[2]),
        pltpu.make_async_copy(basis_hbm, basis, local_sem.at[3]),
    ]
    for load in loads:
        load.start()
    half[0] = jnp.zeros((128, 128), BF)
    sums[CHUNKS] = jnp.zeros((128, 128), F32)
    loads[0].wait()
    pl.semaphore_wait(barrier, 38)

    copies = []

    def push(src, to):
        i = len(copies)
        copy = remote(src, src, ag_send.at[i], ag_recv.at[i], to)
        copy.start()
        copies.append(copy)
        return copy

    along_z = [push(mine, z_peers[k]) for k in (3, 2, 4, 1, 5, 0, 6)]

    *tables, over = sort_terms(
        tl_ref[...], tr_ref[...], ts_ref[...], tt_ref[...], count_ref[0], x, y, plan
    )
    for i, table in enumerate(tables):
        tab_v[i] = table
    to_smem = pltpu.make_async_copy(tab_v, tab_s, local_sem.at[4])
    to_smem.start()

    def even(buf, dx, dy):
        return buf.at[(x + dx) % 4, (y + dy) % 4, c, 0]

    def odd(buf, dx, dy):
        return buf.at[(x + dx) % 4, (y + dy) % 4, c, 1]

    relays = []

    def relay(view):
        relays.append(push(view, twin))

    def push_to(src, dst, to):
        i = len(copies)
        copy = remote(src, dst, ag_send.at[i], ag_recv.at[i], to)
        copy.start()
        copies.append(copy)
        return copy

    def spread_even(d):
        dst = even(xb2 if d else xb1, 0, d)
        src = even(xb1, 0, d)
        return push_to(src, dst, x_peers[0]), push_to(src, dst, x_peers[2])

    def spread_odd(d):
        dst = odd(xb2 if d else xb1, d, 0)
        src = odd(xb1, d, 0)
        return push_to(src, dst, y_peers[0]), push_to(src, dst, y_peers[2])

    def forward_even(d, pair):
        buf = xb2 if d else xb1
        for copy in pair:
            copy.wait_recv()
        relay(even(buf, 3, d))
        relay(even(buf, 1, d))
        step = jnp.where((y + d) % 2 == 0, 3, 1)
        return push_to(even(buf, step, d), even(xb3, step, d), at((x + 4 - step) % 4, y, c, z))

    def forward_odd(d, pair):
        buf = xb2 if d else xb1
        for copy in pair:
            copy.wait_recv()
        relay(odd(buf, d, 3))
        relay(odd(buf, d, 1))
        step = jnp.where((x + d) % 2 == 0, 3, 1)
        return push_to(odd(buf, d, step), odd(xb3, d, step), at(x, (y + 4 - step) % 4, c, z))

    for copy in along_z:
        copy.wait_recv()
    y_even = {k: push(even(xb1, 0, 0), y_peers[k - 1]) for k in (1, 3)}
    x_odd = {k: push(odd(xb1, 0, 0), x_peers[k - 1]) for k in (1, 3)}
    evens, odds = {0: spread_even(0)}, {0: spread_odd(0)}
    y_even[2] = push(even(xb1, 0, 0), y_peers[1])
    x_odd[2] = push(odd(xb1, 0, 0), x_peers[1])
    relay(xb1.at[x, y, c])
    for k in (1, 3):
        y_even[k].wait_recv()
        evens[4 - k] = spread_even(4 - k)
        relay(even(xb1, 0, 4 - k))
        x_odd[k].wait_recv()
        odds[4 - k] = spread_odd(4 - k)
        relay(odd(xb1, 4 - k, 0))
    farthest = {0: (forward_even(0, evens[0]), forward_odd(0, odds[0]))}
    y_even[2].wait_recv()
    evens[2] = spread_even(2)
    relay(even(xb1, 0, 2))
    x_odd[2].wait_recv()
    odds[2] = spread_odd(2)
    relay(odd(xb1, 2, 0))
    to_smem.wait()
    for load in loads[1:]:
        load.wait()

    def products(first, count, steps, buf):
        unroll = count // steps

        def step(i, carry):
            for u in range(unroll):
                slot = first + i * unroll + u
                word = tab_s[0, slot >> 7, slot & 127]
                l, s = word & 63, word >> 6
                block = buf[s >> 4, (s >> 2) & 3, (s >> 1) & 1, s & 1]
                half[slot + 1] = jnp.dot(left[l], block, preferred_element_type=F32).astype(BF)
            return carry

        if count:
            lax.fori_loop(0, steps, step, 0)

    def relayed():
        for copy in relays:
            copy.wait_recv()
        relays.clear()

    kept = []

    def keep_on(src, dst, parts):
        for part_of in parts:
            copy = pltpu.make_async_copy(
                part_of(src), part_of(dst), local_sem.at[5 + len(kept)]
            )
            copy.start()
            kept.append(copy)

    crossing = [lambda b: b.at[x, :, :, 0], lambda b: b.at[:, y, :, 1]]
    beside = [lambda b, d=d: b.at[(x + d) % 4, y, :, 0] for d in (1, 3)]
    beside += [lambda b, d=d: b.at[x, (y + d) % 4, :, 1] for d in (1, 3)]
    flanks = [lambda b, d=d: b.at[(x + d) % 4, :, :, 0] for d in (1, 3)]
    flanks += [lambda b, d=d: b.at[:, (y + d) % 4, :, 1] for d in (1, 3)]

    relayed()
    keep_on(xb1, xb2, crossing + beside)
    products(0, stages[0], 2, xb1)
    for d in (3, 1, 2):
        farthest[d] = (forward_even(d, evens[d]), forward_odd(d, odds[d]))
    relayed()
    for copy in kept:
        copy.wait()
    keep_on(xb2, xb3, crossing + flanks)
    early = stages[1] * 9 // 13 // 8 * 8
    products(stages[0], early, 2, xb2)
    for d in (0, 3, 1, 2):
        for copy in farthest[d]:
            copy.wait_recv()
        relay(even(xb3, 2, d))
        relay(odd(xb3, d, 2))
    products(stages[0] + early, stages[1] - early, 1, xb2)
    relayed()
    for copy in kept[6:]:
        copy.wait()
    products(stages[0] + stages[1], stages[2], 8 if stages[2] > 512 else 2, xb3)

    def chunk_sums(first, unroll, i, acc):
        for v in range(unroll):
            chunk = first + i * unroll + v
            words = []
            for k in range(CHUNK):
                slot = chunk * CHUNK + k
                words.append(tab_s[1 + (slot >> 10), (slot >> 7) & 7, slot & 127])
            halves = jnp.concatenate([half[w & 2047] for w in words], axis=1)
            rights = jnp.concatenate([right[w >> 11] for w in words], axis=1)
            prod = lax.dot_general(halves, rights, NT, preferred_element_type=F32)
            keep = tab_s[3, chunk >> 7, chunk & 127]
            acc = acc * keep.astype(F32) + prod
            sums[chunk] = acc
        return acc

    def send_parts(p):
        for h in range(2):
            total = sums[tab_s[3, 2, 2 * p + h]]
            sig[2 * p + h] = total
            part[p, 4 * h : 4 * h + 4] = total.astype(BF).reshape(4, 32, 128)
        for k in range(8):
            xo, co = (x + k // 2) % 4, (c + k) % 2
            yo = (p - xo + 4) % 4
            owner = (xo * 4 + yo) * 2 + co
            index = (op - owner + 31) % 32
            copy = remote(
                part.at[p, xo * 2 + co],
                inbox.at[index],
                rs_send,
                rs_recv,
                {"op": owner, "sec": z},
            )
            if k == 0:
                pl.when(owner != op)(copy.start)
            else:
                copy.start()

    p_me, m_me = (x + y) % 4, x * 2 + c
    t_me, r_me = 2 * p_me + m_me // 4, pl.multiple_of((m_me % 4) * 32, 32)
    out_mine = outbox.at[t_me, pl.ds(r_me, 32)]
    whole = remote(inbox, inbox, rs_send, rs_recv, twin)
    to_out = [
        remote(out_mine, out_mine, out_send.at[k], out_recv.at[k], peer)
        for k, peer in enumerate(plane)
    ]

    def send_sum():
        whole.wait_recv()
        total = part[p_me, m_me].astype(F32)
        for k in range(31):
            total = total + inbox[k].astype(F32)
        out_mine[...] = total.astype(BF)
        for copy in to_out:
            copy.start()

    def inner(p, sums_k):
        new = []
        for k in range(4):
            acc = sums_k[k]
            for b in (2 * p, 2 * p + 1):
                prod = basis[k, b].astype(F32) * sig[b]
                acc = acc + jnp.sum(prod.reshape(16, 8, 128), axis=0)
            new.append(acc)
        return new

    acc = jnp.zeros((128, 128), F32)
    dots = [jnp.zeros((8, 128), F32) for _ in range(4)]
    for p in range(4):
        first = marks[p - 1] if p else 0
        count = marks[p] - first
        if count:
            steps = 8 if count > 64 else 2
            acc = lax.fori_loop(
                0, steps, functools.partial(chunk_sums, first, count // steps), acc
            )
        send_parts(p)
        dots = inner(p, dots)
        if p >= 2:
            pl.when(p_me == p - 2)(send_sum)

    lane = lax.broadcasted_iota(I32, (1, 128), 1)
    line = jnp.where(lane == 4, over.astype(F32), 0.0)
    for k in range(4):
        total = jnp.sum(jnp.sum(dots[k], axis=0, keepdims=True), axis=1, keepdims=True)
        line = line + jnp.where(lane == k, total, 0.0)
    corr_z[z] = line
    to_z = []
    for k, peer in enumerate(z_peers):
        copy = remote(corr_z.at[z], corr_z.at[z], cz_send.at[k], cz_recv.at[k], peer)
        copy.start()
        to_z.append(copy)

    pl.when(p_me == 2)(send_sum)
    pl.when(p_me == 3)(send_sum)

    for copy in to_z:
        copy.wait_recv()
    z_sum = corr_z[0]
    for k in range(1, 8):
        z_sum = z_sum + corr_z[k]
    corr_p[op] = z_sum
    to_plane = []
    for k, peer in enumerate(plane):
        copy = remote(corr_p.at[op], corr_p.at[op], cp_send.at[k], cp_recv.at[k], peer)
        copy.start()
        to_plane.append(copy)

    for copy in to_out:
        copy.wait_recv()
    sigma_ref[...] = outbox[...].astype(F32)
    for copy in to_plane:
        copy.wait_recv()
    p_sum = corr_p[0]
    for k in range(1, 32):
        p_sum = p_sum + corr_p[k]
    for k in range(4):
        corr_ref[k] = jnp.sum(jnp.where(lane == k, p_sum, 0.0))
    over_ref[0] = jnp.sum(jnp.where(lane == 4, p_sum, 0.0))

    for copy in copies + to_z + to_out + to_plane:
        copy.wait_send()
    whole.wait_send()


def run(plan, which, arrays):
    vmem = pl.BlockSpec(memory_space=pltpu.VMEM)
    smem = pl.BlockSpec(memory_space=pltpu.SMEM)
    hbm = pl.BlockSpec(memory_space=pltpu.HBM)
    dma = pltpu.SemaphoreType.DMA
    return pl.pallas_call(
        functools.partial(kernel, plan),
        out_shape=(
            jax.ShapeDtypeStruct((8, 128, 128), F32),
            jax.ShapeDtypeStruct((4,), F32),
            jax.ShapeDtypeStruct((1,), F32),
        ),
        in_specs=[vmem, hbm, hbm, hbm, vmem, vmem, vmem, vmem, smem],
        out_specs=(vmem, smem, smem),
        scratch_shapes=[
            pltpu.VMEM((4, 4, 2, 2, 128, 128), BF),
            pltpu.VMEM((4, 4, 2, 2, 128, 128), BF),
            pltpu.VMEM((4, 4, 2, 2, 128, 128), BF),
            pltpu.VMEM((64, 128, 128), BF),
            pltpu.VMEM((64, 128, 128), BF),
            pltpu.VMEM((4, 8, 128, 128), BF),
            pltpu.VMEM((SLOTS + 1, 128, 128), BF),
            pltpu.VMEM((CHUNKS + 1, 128, 128), F32),
            pltpu.VMEM((4, 8, 128), I32),
            pltpu.SMEM((4, 8, 128), I32),
            pltpu.VMEM((8, 128, 128), F32),
            pltpu.VMEM((4, 8, 32, 128), BF),
            pltpu.VMEM((31, 32, 128), BF),
            pltpu.VMEM((8, 128, 128), BF),
            pltpu.VMEM((8, 1, 128), F32),
            pltpu.VMEM((32, 1, 128), F32),
            dma((17,)),
            dma((80,)),
            dma((80,)),
            dma(()),
            dma(()),
            dma((31,)),
            dma((31,)),
            dma((7,)),
            dma((7,)),
            dma((31,)),
            dma((31,)),
        ],
        compiler_params=pltpu.CompilerParams(
            collective_id=which, has_side_effects=True, vmem_limit_bytes=60 * 1024 * 1024
        ),
    )(*arrays)


def body(wavefunction, left_ops, right_ops, basis, tl, tr, ts, tt, count):
    terms = (t.reshape(8, 128) for t in (tl, tr, ts, tt))
    arrays = (wavefunction, left_ops, right_ops, basis, *terms, count)
    sigma, corr, over = run(STAGED, 0, arrays)
    return lax.cond(
        over[0] > 0, lambda: tuple(run(GENERAL, 1, arrays)[:2]), lambda: (sigma, corr)
    )


def solution(mesh):
    placed = (
        P(("op", "sec"), None),
        P(("op", "sec"), None, None),
        P(("op", "sec"), None, None),
        P(None, "sec", None, None),
        P(("op", "sec")),
        P(("op", "sec")),
        P(("op", "sec")),
        P(("op", "sec")),
        P(("op", "sec")),
    )
    return jax.shard_map(
        body, mesh=mesh, in_specs=placed, out_specs=(P("sec", None, None), P()), check_vma=False
    )
```

time: 71.2 us -> 66.2 us (0.930)
  Pallas kernels: 66.6 us -> 61.6 us
  other arithmetic: 1.78 us -> 0 us
  local copies, waits for them, and re-layouts: 1.3 us -> 2.41 us
  between operations: 1.29 us -> 2.04 us
    pallas_call x1, Pallas kernels: 66.6 us -> 61.6 us  [run(): pl.pallas_call(functools.partial(kernel, plan), out_shape=(jax.ShapeDtype...]
    unnamed x0 -> x16, local copies, waits for them, and re-layouts: none -> 2.41 us
    convert_element_type x1 -> x0, other arithmetic: 1.78 us -> none  [body(): return (sigma.astype(F32), corr[:4, 0])]
    slice x1 -> x0, local copies, waits for them, and re-layouts: 1.3 us -> none  [body(): return (sigma.astype(F32), corr[:4, 0])]
where the time goes in v2:
time: 66.2 us; the launch traced here: 66.1 us
  Pallas kernels  61.6 us (93%)
  local copies, waits for them, and re-layouts  2.41 us (4%)
  between operations  2.04 us (3%)
    pallas_call x1, Pallas kernels, run(): pl.pallas_call(functools.partial(kernel, plan), out_shape=(jax.ShapeDtype...  61.6 us
    unnamed x16, local copies, waits for them, and re-layouts  2.41 us

profile of v2, /device:TPU:1, one launch (start us, length us, event | category | flops | bytes accessed | tf_op | source)
XLA Modules:
  0.0 66.1 jit_solution(15681912180005714731)
XLA Ops:
  1.3 0.0 copy-start
  1.3 0.0 copy-start.1
  1.3 0.0 copy-start.2
  1.3 0.0 copy-start.3
  1.3 0.0 copy-start.4
  1.3 0.0 copy-start.5
  1.3 0.0 copy-start.6
  1.3 61.6 %shard_map.108 = (f32[8,128,128]{2,1,0:T(8,128)}, f32[4]{0:T(128)S(1)}, f32[1]{0:T(128)}) custom-call(bf16[32,128]{1,0:T(8,128)(2,1)} %w_ref.1, bf16[64,128,128]{2,1,0:T(8,128)(2,1)} %left_hbm.1, bf16[64,128,128]{2,1,0:T(8,128)(2,1)} %right_hbm.1, bf16[4,8,128,128]{3,2,1,0:T(8,128)(2,1)} %basis_hbm.1, s32[8,128]{1,0:T(8,128)} %bitcast.5, s32[8,128]{1,0:T(8,128)} %bitcast.7, ...), custom_call_target="tpu_custom_call" | custom-call | tf_op jit(solution)/shard_map/pallas_call | solution.py:457
  63.6 0.0 copy-done
  63.6 0.0 copy-done.1
  63.6 0.0 copy-done.2
  63.6 0.0 copy-done.3
  63.6 0.0 copy-done.4
  63.7 0.0 copy-done.5
  63.7 0.0 copy-done.6
  63.7 1.9 %copy.22 = f32[8,128,128]{2,1,0:T(8,128)} copy(f32[8,128,128]{2,1,0:T(8,128)} %get-tuple-element.51) | data formatting | bytes 1048576
  65.6 0.5 copy.23
  (1 shorter events, 0.0 us)
Async XLA Ops:
  1.3 62.3 %copy-start = (bf16[64,128,128]{2,1,0:T(8,128)(2,1)S(1)}, bf16[64,128,128]{2,1,0:T(8,128)(2,1)}, u32[]{:S(2)}) copy-start(bf16[64,128,128]{2,1,0:T(8,128)(2,1)} %left_hbm.1) | copy-start | bytes 6291460
  1.3 62.3 %copy-start.1 = (bf16[4,8,128,128]{3,2,1,0:T(8,128)(2,1)S(1)}, bf16[4,8,128,128]{3,2,1,0:T(8,128)(2,1)}, u32[]{:S(2)}) copy-start(bf16[4,8,128,128]{3,2,1,0:T(8,128)(2,1)} %basis_hbm.1) | copy-start | bytes 3145732
  1.3 62.3 %copy-start.2 = (bf16[32,128]{1,0:T(8,128)(2,1)S(1)}, bf16[32,128]{1,0:T(8,128)(2,1)}, u32[]{:S(2)}) copy-start(bf16[32,128]{1,0:T(8,128)(2,1)} %w_ref.1) | copy-start | bytes 24580
  1.3 62.3 %copy-start.3 = (s32[1024]{0:T(1024)S(1)}, s32[1024]{0:T(1024)}, u32[]{:S(2)}) copy-start(s32[1024]{0:T(1024)} %param.15) | copy-start | bytes 12292
  1.3 62.3 %copy-start.4 = (s32[1024]{0:T(1024)S(1)}, s32[1024]{0:T(1024)}, u32[]{:S(2)}) copy-start(s32[1024]{0:T(1024)} %param.16) | copy-start | bytes 12292
  1.3 62.3 %copy-start.5 = (s32[1024]{0:T(1024)S(1)}, s32[1024]{0:T(1024)}, u32[]{:S(2)}) copy-start(s32[1024]{0:T(1024)} %param.17) | copy-start | bytes 12292
  1.3 62.3 %copy-start.6 = (s32[1024]{0:T(1024)S(1)}, s32[1024]{0:T(1024)}, u32[]{:S(2)}) copy-start(s32[1024]{0:T(1024)} %param.18) | copy-start | bytes 12292

commit v3 on v2

--- a/solution.py
+++ b/solution.py
@@ -133,6 +133,8 @@
     corr_z,
     corr_p,
     local_sem,
+    relay_send,
+    relay_recv,
     ag_send,
     ag_recv,
     rs_send,
@@ -201,10 +203,8 @@
     def odd(buf, dx, dy):
         return buf.at[(x + dx) % 4, (y + dy) % 4, c, 1]
 
-    relays = []
-
-    def relay(view):
-        relays.append(push(view, twin))
+    def relay(view, stage):
+        remote(view, view, relay_send, relay_recv.at[stage], twin).start()
 
     def push_to(src, dst, to):
         i = len(copies)
@@ -227,8 +227,8 @@
         buf = xb2 if d else xb1
         for copy in pair:
             copy.wait_recv()
-        relay(even(buf, 3, d))
-        relay(even(buf, 1, d))
+        relay(even(buf, 3, d), 1 if d else 0)
+        relay(even(buf, 1, d), 1 if d else 0)
         step = jnp.where((y + d) % 2 == 0, 3, 1)
         return push_to(even(buf, step, d), even(xb3, step, d), at((x + 4 - step) % 4, y, c, z))
 
@@ -236,8 +236,8 @@
         buf = xb2 if d else xb1
         for copy in pair:
             copy.wait_recv()
-        relay(odd(buf, d, 3))
-        relay(odd(buf, d, 1))
+        relay(odd(buf, d, 3), 1 if d else 0)
+        relay(odd(buf, d, 1), 1 if d else 0)
         step = jnp.where((x + d) % 2 == 0, 3, 1)
         return push_to(odd(buf, d, step), odd(xb3, d, step), at(x, (y + 4 - step) % 4, c, z))
 
@@ -248,21 +248,21 @@
     evens, odds = {0: spread_even(0)}, {0: spread_odd(0)}
     y_even[2] = push(even(xb1, 0, 0), y_peers[1])
     x_odd[2] = push(odd(xb1, 0, 0), x_peers[1])
-    relay(xb1.at[x, y, c])
+    relay(xb1.at[x, y, c], 0)
     for k in (1, 3):
         y_even[k].wait_recv()
         evens[4 - k] = spread_even(4 - k)
-        relay(even(xb1, 0, 4 - k))
+        relay(even(xb1, 0, 4 - k), 0)
         x_odd[k].wait_recv()
         odds[4 - k] = spread_odd(4 - k)
-        relay(odd(xb1, 4 - k, 0))
+        relay(odd(xb1, 4 - k, 0), 0)
     farthest = {0: (forward_even(0, evens[0]), forward_odd(0, odds[0]))}
     y_even[2].wait_recv()
     evens[2] = spread_even(2)
-    relay(even(xb1, 0, 2))
+    relay(even(xb1, 0, 2), 0)
     x_odd[2].wait_recv()
     odds[2] = spread_odd(2)
-    relay(odd(xb1, 2, 0))
+    relay(odd(xb1, 2, 0), 0)
     to_smem.wait()
     for load in loads[1:]:
         load.wait()
@@ -282,10 +282,11 @@
         if count:
             lax.fori_loop(0, steps, step, 0)
 
-    def relayed():
-        for copy in relays:
-            copy.wait_recv()
-        relays.clear()
+    sizes = (xb1.at[0, pl.ds(0, 3)], xb2.at[0, pl.ds(0, 3)], xb3.at[0, pl.ds(0, 2)])
+
+    def relayed(stage):
+        view = sizes[stage]
+        remote(view, view, relay_send, relay_recv.at[stage], twin).wait_recv()
 
     kept = []
 
@@ -303,12 +304,12 @@
     flanks = [lambda b, d=d: b.at[(x + d) % 4, :, :, 0] for d in (1, 3)]
     flanks += [lambda b, d=d: b.at[:, (y + d) % 4, :, 1] for d in (1, 3)]
 
-    relayed()
+    relayed(0)
     keep_on(xb1, xb2, crossing + beside)
     products(0, stages[0], 2, xb1)
     for d in (3, 1, 2):
         farthest[d] = (forward_even(d, evens[d]), forward_odd(d, odds[d]))
-    relayed()
+    relayed(1)
     for copy in kept:
         copy.wait()
     keep_on(xb2, xb3, crossing + flanks)
@@ -317,10 +318,10 @@
     for d in (0, 3, 1, 2):
         for copy in farthest[d]:
             copy.wait_recv()
-        relay(even(xb3, 2, d))
-        relay(odd(xb3, d, 2))
+        relay(even(xb3, 2, d), 2)
+        relay(odd(xb3, d, 2), 2)
     products(stages[0] + early, stages[1] - early, 1, xb2)
-    relayed()
+    relayed(2)
     for copy in kept[6:]:
         copy.wait()
     products(stages[0] + stages[1], stages[2], 8 if stages[2] > 512 else 2, xb3)
@@ -367,8 +368,8 @@
     out_mine = outbox.at[t_me, pl.ds(r_me, 32)]
     whole = remote(inbox, inbox, rs_send, rs_recv, twin)
     to_out = [
-        remote(out_mine, out_mine, out_send.at[k], out_recv.at[k], peer)
-        for k, peer in enumerate(plane)
+        remote(out_mine, out_mine, out_send, out_recv, peer)
+        for peer in plane
     ]
 
     def send_sum():
@@ -380,30 +381,33 @@
         for copy in to_out:
             copy.start()
 
-    def inner(p, sums_k):
+    def inner(b, dots):
         new = []
         for k in range(4):
-            acc = sums_k[k]
-            for b in (2 * p, 2 * p + 1):
-                prod = basis[k, b].astype(F32) * sig[b]
-                acc = acc + jnp.sum(prod.reshape(16, 8, 128), axis=0)
-            new.append(acc)
+            prod = basis[k, b].astype(F32) * sig[b]
+            new.append(dots[k] + jnp.sum(prod.reshape(16, 8, 128), axis=0))
         return new
 
-    acc = jnp.zeros((128, 128), F32)
-    dots = [jnp.zeros((8, 128), F32) for _ in range(4)]
+    def segment(first, unroll, ready, i, carry):
+        acc, dots = carry[0], list(carry[1:])
+        if ready is not None:
+            dots = inner(2 * ready + i, dots)
+        return (chunk_sums(first, unroll, i, acc), *dots)
+
+    carry = (jnp.zeros((128, 128), F32), *(jnp.zeros((8, 128), F32) for _ in range(4)))
     for p in range(4):
         first = marks[p - 1] if p else 0
         count = marks[p] - first
+        ready = p - 1 if p else None
         if count:
             steps = 8 if count > 64 else 2
-            acc = lax.fori_loop(
-                0, steps, functools.partial(chunk_sums, first, count // steps), acc
-            )
+            step = functools.partial(segment, first, count // steps, ready)
+            carry = lax.fori_loop(0, steps, step, carry)
+        elif p:
+            dots = inner(2 * ready + 1, inner(2 * ready, list(carry[1:])))
+            carry = (carry[0], *dots)
         send_parts(p)
-        dots = inner(p, dots)
-        if p >= 2:
-            pl.when(p_me == p - 2)(send_sum)
+    dots = inner(7, inner(6, list(carry[1:])))
 
     lane = lax.broadcasted_iota(I32, (1, 128), 1)
     line = jnp.where(lane == 4, over.astype(F32), 0.0)
@@ -411,32 +415,33 @@
         total = jnp.sum(jnp.sum(dots[k], axis=0, keepdims=True), axis=1, keepdims=True)
         line = line + jnp.where(lane == k, total, 0.0)
     corr_z[z] = line
-    to_z = []
-    for k, peer in enumerate(z_peers):
-        copy = remote(corr_z.at[z], corr_z.at[z], cz_send.at[k], cz_recv.at[k], peer)
-        copy.start()
-        to_z.append(copy)
-
+    for peer in z_peers:
+        remote(corr_z.at[z], corr_z.at[z], cz_send, cz_recv, peer).start()
+
+    pl.when(p_me == 0)(send_sum)
+    pl.when(p_me == 1)(send_sum)
+    for copy in copies:
+        copy.wait_send()
+    remote(xb1.at[pl.ds(0, 2)], xb1.at[pl.ds(0, 2)], relay_send, relay_recv.at[0], twin).wait_send()
     pl.when(p_me == 2)(send_sum)
     pl.when(p_me == 3)(send_sum)
 
-    for copy in to_z:
-        copy.wait_recv()
+    z_rows = corr_z.at[pl.ds(0, 7)]
+    from_z = remote(z_rows, z_rows, cz_send, cz_recv, twin)
+    from_z.wait_recv()
     z_sum = corr_z[0]
     for k in range(1, 8):
         z_sum = z_sum + corr_z[k]
     corr_p[op] = z_sum
-    to_plane = []
-    for k, peer in enumerate(plane):
-        copy = remote(corr_p.at[op], corr_p.at[op], cp_send.at[k], cp_recv.at[k], peer)
-        copy.start()
-        to_plane.append(copy)
-
-    for copy in to_out:
-        copy.wait_recv()
+    for peer in plane:
+        remote(corr_p.at[op], corr_p.at[op], cp_send, cp_recv, peer).start()
+
+    out_all = remote(inbox, inbox, out_send, out_recv, twin)
+    out_all.wait_recv()
     sigma_ref[...] = outbox[...].astype(F32)
-    for copy in to_plane:
-        copy.wait_recv()
+    p_rows = corr_p.at[pl.ds(0, 31)]
+    from_plane = remote(p_rows, p_rows, cp_send, cp_recv, twin)
+    from_plane.wait_recv()
     p_sum = corr_p[0]
     for k in range(1, 32):
         p_sum = p_sum + corr_p[k]
@@ -444,9 +449,8 @@
         corr_ref[k] = jnp.sum(jnp.where(lane == k, p_sum, 0.0))
     over_ref[0] = jnp.sum(jnp.where(lane == 4, p_sum, 0.0))
 
-    for copy in copies + to_z + to_out + to_plane:
+    for copy in (whole, from_z, out_all, from_plane):
         copy.wait_send()
-    whole.wait_send()
 
 
 def run(plan, which, arrays):
@@ -481,19 +485,21 @@
             pltpu.VMEM((8, 1, 128), F32),
             pltpu.VMEM((32, 1, 128), F32),
             dma((17,)),
+            dma(()),
+            dma((3,)),
             dma((80,)),
             dma((80,)),
             dma(()),
             dma(()),
-            dma((31,)),
-            dma((31,)),
-            dma((7,)),
-            dma((7,)),
-            dma((31,)),
-            dma((31,)),
+            dma(()),
+            dma(()),
+            dma(()),
+            dma(()),
+            dma(()),
+            dma(()),
         ],
         compiler_params=pltpu.CompilerParams(
-            collective_id=which, has_side_effects=True, vmem_limit_bytes=60 * 1024 * 1024
+            collective_id=which, has_side_effects=True, vmem_limit_bytes=63 * 1024 * 1024
         ),
     )(*arrays)
 

time: 66.2 us -> 63.8 us (0.964)
  Pallas kernels: 61.6 us -> 60.3 us
  local copies, waits for them, and re-layouts: 2.41 us -> 1.33 us
    pallas_call x1, Pallas kernels: 61.6 us -> 60.3 us  [run(): pl.pallas_call(functools.partial(kernel, plan), out_shape=(jax.ShapeDtype...]
    unnamed x16 -> x12, local copies, waits for them, and re-layouts: 2.41 us -> 1.33 us
where the time goes in v3:
time: 63.8 us; the launch traced here: 63.6 us
  Pallas kernels  60.3 us (95%)
  between operations  2 us (3%)
  local copies, waits for them, and re-layouts  1.33 us (2%)
    pallas_call x1, Pallas kernels, run(): pl.pallas_call(functools.partial(kernel, plan), out_shape=(jax.ShapeDtype...  60.3 us
    unnamed x12, local copies, waits for them, and re-layouts  1.33 us

profile of v3, /device:TPU:1, one launch (start us, length us, event | category | flops | bytes accessed | tf_op | source)
XLA Modules:
  0.0 63.6 jit_solution(17444059826573009331)
XLA Ops:
  1.3 0.0 copy-start
  1.3 0.0 copy-start.1
  1.3 0.0 copy-start.2
  1.3 0.0 copy-start.3
  1.3 0.0 copy-start.4
  1.3 60.3 %shard_map.108 = (f32[8,128,128]{2,1,0:T(8,128)S(1)}, f32[4]{0:T(128)S(1)}, f32[1]{0:T(128)}) custom-call(bf16[32,128]{1,0:T(8,128)(2,1)} %w_ref.1, bf16[64,128,128]{2,1,0:T(8,128)(2,1)} %left_hbm.1, bf16[64,128,128]{2,1,0:T(8,128)(2,1)} %right_hbm.1, bf16[4,8,128,128]{3,2,1,0:T(8,128)(2,1)} %basis_hbm.1, s32[8,128]{1,0:T(8,128)} %bitcast.5, ...), custom_call_target="tpu_custom_call" | custom-call | tf_op jit(solution)/shard_map/pallas_call | solution.py:461
  62.3 0.0 copy-done
  62.3 0.0 copy-done.1
  62.3 0.0 copy-done.2
  62.3 0.0 copy-done.3
  62.3 0.0 copy-done.4
  62.3 0.8 %copy.22 = f32[8,128,128]{2,1,0:T(8,128)} copy(f32[8,128,128]{2,1,0:T(8,128)S(1)} %get-tuple-element.51) | data formatting | bytes 1048576
  63.1 0.5 copy.23
  (1 shorter events, 0.0 us)
Async XLA Ops:
  1.3 61.0 %copy-start = (bf16[32,128]{1,0:T(8,128)(2,1)S(1)}, bf16[32,128]{1,0:T(8,128)(2,1)}, u32[]{:S(2)}) copy-start(bf16[32,128]{1,0:T(8,128)(2,1)} %w_ref.1) | copy-start | bytes 24580
  1.3 61.0 %copy-start.1 = (s32[1024]{0:T(1024)S(1)}, s32[1024]{0:T(1024)}, u32[]{:S(2)}) copy-start(s32[1024]{0:T(1024)} %param.15) | copy-start | bytes 12292
  1.3 61.0 %copy-start.2 = (s32[1024]{0:T(1024)S(1)}, s32[1024]{0:T(1024)}, u32[]{:S(2)}) copy-start(s32[1024]{0:T(1024)} %param.16) | copy-start | bytes 12292
  1.3 61.0 %copy-start.3 = (s32[1024]{0:T(1024)S(1)}, s32[1024]{0:T(1024)}, u32[]{:S(2)}) copy-start(s32[1024]{0:T(1024)} %param.17) | copy-start | bytes 12292
  1.3 61.0 %copy-start.4 = (s32[1024]{0:T(1024)S(1)}, s32[1024]{0:T(1024)}, u32[]{:S(2)}) copy-start(s32[1024]{0:T(1024)} %param.18) | copy-start | bytes 12292

commit v4 on v3

--- a/solution.py
+++ b/solution.py
@@ -160,7 +160,7 @@
     twin = at(x, y, 1 - c, z)
 
     barrier = pltpu.get_barrier_semaphore()
-    for peer in z_peers + plane:
+    for peer in z_peers + y_peers + x_peers + [twin]:
         pl.semaphore_signal(barrier, inc=1, device_id=peer, device_id_type=MESH)
 
     stages, marks = plan
@@ -176,7 +176,7 @@
     half[0] = jnp.zeros((128, 128), BF)
     sums[CHUNKS] = jnp.zeros((128, 128), F32)
     loads[0].wait()
-    pl.semaphore_wait(barrier, 38)
+    pl.semaphore_wait(barrier, 14)
 
     copies = []
 

time: 63.8 us -> 62.9 us (0.986)
  Pallas kernels: 60.3 us -> 59.4 us
    pallas_call x1, Pallas kernels: 60.3 us -> 59.4 us  [run(): pl.pallas_call(functools.partial(kernel, plan), out_shape=(jax.ShapeDtype...]
where the time goes in v4:
time: 62.9 us; the launch traced here: 62.7 us
  Pallas kernels  59.4 us (94%)
  between operations  2 us (3%)
  local copies, waits for them, and re-layouts  1.33 us (2%)
    pallas_call x1, Pallas kernels, run(): pl.pallas_call(functools.partial(kernel, plan), out_shape=(jax.ShapeDtype...  59.4 us
    unnamed x12, local copies, waits for them, and re-layouts  1.33 us

profile of v4, /device:TPU:1, one launch (start us, length us, event | category | flops | bytes accessed | tf_op | source)
XLA Modules:
  0.0 62.7 jit_solution(15511045117031353190)
XLA Ops:
  1.3 0.0 copy-start
  1.3 0.0 copy-start.1
  1.3 0.0 copy-start.2
  1.3 0.0 copy-start.3
  1.3 0.0 copy-start.4
  1.3 59.4 %shard_map.108 = (f32[8,128,128]{2,1,0:T(8,128)S(1)}, f32[4]{0:T(128)S(1)}, f32[1]{0:T(128)}) custom-call(bf16[32,128]{1,0:T(8,128)(2,1)} %w_ref.1, bf16[64,128,128]{2,1,0:T(8,128)(2,1)} %left_hbm.1, bf16[64,128,128]{2,1,0:T(8,128)(2,1)} %right_hbm.1, bf16[4,8,128,128]{3,2,1,0:T(8,128)(2,1)} %basis_hbm.1, s32[8,128]{1,0:T(8,128)} %bitcast.5, ...), custom_call_target="tpu_custom_call" | custom-call | tf_op jit(solution)/shard_map/pallas_call | solution.py:461
  61.4 0.0 copy-done
  61.4 0.0 copy-done.1
  61.4 0.0 copy-done.2
  61.4 0.0 copy-done.3
  61.4 0.0 copy-done.4
  61.4 0.8 %copy.22 = f32[8,128,128]{2,1,0:T(8,128)} copy(f32[8,128,128]{2,1,0:T(8,128)S(1)} %get-tuple-element.51) | data formatting | bytes 1048576
  62.2 0.5 copy.23
  (1 shorter events, 0.0 us)
Async XLA Ops:
  1.3 60.1 %copy-start = (bf16[32,128]{1,0:T(8,128)(2,1)S(1)}, bf16[32,128]{1,0:T(8,128)(2,1)}, u32[]{:S(2)}) copy-start(bf16[32,128]{1,0:T(8,128)(2,1)} %w_ref.1) | copy-start | bytes 24580
  1.3 60.1 %copy-start.1 = (s32[1024]{0:T(1024)S(1)}, s32[1024]{0:T(1024)}, u32[]{:S(2)}) copy-start(s32[1024]{0:T(1024)} %param.15) | copy-start | bytes 12292
  1.3 60.1 %copy-start.2 = (s32[1024]{0:T(1024)S(1)}, s32[1024]{0:T(1024)}, u32[]{:S(2)}) copy-start(s32[1024]{0:T(1024)} %param.16) | copy-start | bytes 12292
  1.3 60.1 %copy-start.3 = (s32[1024]{0:T(1024)S(1)}, s32[1024]{0:T(1024)}, u32[]{:S(2)}) copy-start(s32[1024]{0:T(1024)} %param.17) | copy-start | bytes 12292
  1.3 60.1 %copy-start.4 = (s32[1024]{0:T(1024)S(1)}, s32[1024]{0:T(1024)}, u32[]{:S(2)}) copy-start(s32[1024]{0:T(1024)} %param.18) | copy-start | bytes 12292
